TPU v7x, 256 devices: a whole 4x4x8 slice. The times are simulated.
256 devices in a mesh: gx: 128 (over x_lo, y, z, core), gy: 2 (over x_hi).
Axes of the slice: x: 4 (x_hi: 2, x_lo: 2; x = x_hi * 2 + x_lo), y: 4, z: 8, core: 2. Of those that a mesh axis runs over, the one named last changes fastest.
Arguments:
- velocity: float32 [3, 512, 32, 128], P(None, 'gx', 'gy'), may hold values from -6 to 6
- kernel_in: bfloat16 [64, 3, 3, 3, 3], replicated, may hold values from -0.625 to 0.625
- kernel_mid: bfloat16 [64, 64, 3, 3, 3], replicated, may hold values from -0.15625 to 0.15625
- kernel_out: bfloat16 [6, 64, 3, 3, 3], replicated, may hold values from -0.15625 to 0.15625
Outputs:
- tendency: float32 [3, 512, 32, 128], P(None, 'gx', 'gy')
- stress: float32 [6, 512, 32, 128], P(None, 'gx', 'gy')
All inputs are finite; a program needn't handle non-finite values.
Results may differ from a plain program's by a relative error of at most 0.0056.
Values may be sent and summed in bfloat16 or wider, within the bound.
A program may use at most 128 MiB of HBM per device.

v0:
```python
import jax
import jax.numpy as jnp
from jax import lax
from jax.sharding import PartitionSpec as P

FIRST = ((1, 0.75), (2, -0.15), (3, 1.0 / 60.0))
SECOND = ((1, 1.5), (2, -0.15), (3, 1.0 / 90.0))
CENTER = -49.0 / 18.0


def padded(block, sides, width, periodic):
    for axis, dim in sides:
        count = lax.axis_size(axis)
        forward = [(i, i + 1) for i in range(count - 1)]
        if periodic:
            forward.append((count - 1, 0))
        backward = [(target, source) for source, target in forward]
        low = lax.ppermute(
            lax.slice_in_dim(block, block.shape[dim] - width, None, axis=dim), axis, forward
        )
        high = lax.ppermute(lax.slice_in_dim(block, 0, width, axis=dim), axis, backward)
        block = jnp.concatenate([low, block, high], axis=dim)
    return block


def cut(ext, axis, start, count):
    return lax.slice_in_dim(ext, start, start + count, axis=axis)


def first_deriv(ext, axis, count):
    total = 0.0
    for step, coef in FIRST:
        total = total + coef * (cut(ext, axis, 3 + step, count) - cut(ext, axis, 3 - step, count))
    return total


def second_deriv(ext, axis, count):
    total = CENTER * cut(ext, axis, 3, count)
    for step, coef in SECOND:
        total = total + coef * (cut(ext, axis, 3 + step, count) + cut(ext, axis, 3 - step, count))
    return total


def first_span(field):
    total = 0.0
    for step, coef in FIRST:
        total = total + coef * (jnp.roll(field, -step, 3) - jnp.roll(field, step, 3))
    return total


def second_span(field):
    total = CENTER * field
    for step, coef in SECOND:
        total = total + coef * (jnp.roll(field, -step, 3) + jnp.roll(field, step, 3))
    return total


def conv_valid(act, kernel):
    wide = jnp.concatenate([act[..., -1:], act, act[..., :1]], axis=3)
    out = lax.conv_general_dilated(
        wide[None],
        kernel,
        (1, 1, 1),
        "VALID",
        dimension_numbers=("NCDHW", "OIDHW", "NCDHW"),
        preferred_element_type=jnp.float32,
    )
    return out[0]


def activate(values):
    return jax.nn.gelu(values, approximate=True)


def widen(act):
    along = padded(act, (("gx", 1),), 1, True)
    return padded(along, (("gy", 2),), 1, False)


def shards(velocity, kernel_in, kernel_mid, kernel_out):
    rows_x = velocity.shape[1]
    rows_y = velocity.shape[2]
    along_x = padded(velocity, (("gx", 1),), 3, True)
    vel_ext = padded(along_x, (("gy", 2),), 3, False)
    first_in = vel_ext[:, 2:-2, 2:-2, :].astype(jnp.bfloat16)
    hidden1 = activate(conv_valid(first_in, kernel_in)).astype(jnp.bfloat16)
    hidden2 = activate(conv_valid(widen(hidden1), kernel_mid)).astype(jnp.bfloat16)
    stress = conv_valid(widen(hidden2), kernel_out)
    ext_x = vel_ext[:, :, 3:-3, :]
    ext_y = vel_ext[:, 3:-3, :, :]
    grad_x = first_deriv(ext_x, 1, rows_x)
    grad_y = first_deriv(ext_y, 2, rows_y)
    grad_z = first_span(velocity)
    advect = velocity[0][None] * grad_x + velocity[1][None] * grad_y + velocity[2][None] * grad_z
    lap = second_deriv(ext_x, 1, rows_x) + second_deriv(ext_y, 2, rows_y) + second_span(velocity)
    str_x = padded(stress.astype(jnp.bfloat16), (("gx", 1),), 3, True).astype(stress.dtype)
    str_ext = padded(str_x.astype(jnp.bfloat16), (("gy", 2),), 3, False).astype(str_x.dtype)
    parts_x = jnp.stack([str_ext[0], str_ext[3], str_ext[4]])[:, :, 3:-3, :]
    parts_y = jnp.stack([str_ext[3], str_ext[1], str_ext[5]])[:, 3:-3, :, :]
    parts_z = jnp.stack([stress[4], stress[5], stress[2]])
    divergence = (
        first_deriv(parts_x, 1, rows_x) + first_deriv(parts_y, 2, rows_y) + first_span(parts_z)
    )
    tendency = -advect + 0.2 * lap - divergence
    return (tendency, stress)


def solution(mesh):
    placed = (P(None, "gx", "gy", None), P(), P(), P())
    return jax.shard_map(
        shards,
        mesh=mesh,
        in_specs=placed,
        out_specs=(P(None, "gx", "gy", None), P(None, "gx", "gy", None)),
        check_vma=False,
    )
```

profile of v0, /device:TPU:2, one launch (start us, length us, event | category | flops | bytes accessed | tf_op | source)
XLA Modules:
  0.0 347.0 jit_solution(2517674708694077265)
XLA Ops:
  1.8 7.8 %collective-permute-start = (f32[3,3,16,128]{3,2,0,1:T(8,128)S(1)}, f32[3,3,16,128]{3,2,0,1:T(8,128)S(1)}, u32[]{:S(2)}, u32[]{:S(2)}) collective-permute-start(f32[3,3,16,128]{3,2,0,1:T(8,128)S(1)} %copy.145), channel_id=1, source_target_pairs={{2,0},{4,2},{6,4},{8,6},{10,8},{12,10},{14,12},{16,14},{18,16},{20... | collective-permute-start | bytes 221192 | tf_op jit(solution)/shard_map/ppermute | solution.py:21
  12.5 4.3 %collective-permute-start.3 = (f32[3,10,3,128]{3,2,0,1:T(4,128)S(1)}, f32[3,10,3,128]{3,2,0,1:T(4,128)S(1)}, u32[]{:S(2)}, u32[]{:S(2)}) collective-permute-start(f32[3,10,3,128]{3,2,0,1:T(4,128)S(1)} %get-tuple-element.28), channel_id=1, source_target_pairs={{0,1},{2,3},{4,5},{6,7},{8,9},{10,11},{12,13},{14,15},{16,17},{18,... | collective-permute-start | bytes 138248 | tf_op jit(solution)/shard_map/ppermute | solution.py:18
  19.9 4.6 %collective-permute-done.2 = f32[3,10,3,128]{3,2,0,1:T(4,128)S(1)} collective-permute-done((f32[3,10,3,128]{3,2,0,1:T(4,128)S(1)}, f32[3,10,3,128]{3,2,0,1:T(4,128)S(1)}, u32[]{:S(2)}, u32[]{:S(2)}) %collective-permute-start.2) | collective-permute-done | bytes 46112 | tf_op jit(solution)/shard_map/ppermute | solution.py:21
  29.3 8.6 %broadcast_select_fusion.2 = f32[4,16,8,17,64]{4,2,3,1,0:T(8,128)S(1)} fusion(pred[8,17]{0,1:T(8,128)(4,1)S(1)} %copy-done.35, bf16[3,6,18,1,7,2]{4,0,5,2,1,3:T(4,128)(2,1)S(1)} %slice.454, bf16[3,6,18,1,8,17]{4,0,5,2,1,3:T(4,128)(2,1)S(1)} %copy.109, bf16[64,3,3,3,3]{0,4,3,2,1:T(4,128)(2,1)S(1)} %copy-done.34), kind=kOutput, calls=%fused_computation.43 | convolution fusion | flops 91095616 | bytes 2335928 | tf_op jit(solution)/shard_map/conv_general_dilated | solution.py:60
  40.4 6.2 %collective-permute-start.5 = (bf16[64,1,16,128]{0,2,3,1:T(8,128)(2,1)S(1)}, bf16[64,1,16,128]{0,2,3,1:T(8,128)(2,1)S(1)}, u32[]{:S(2)}, u32[]{:S(2)}) collective-permute-start(bf16[64,1,16,128]{0,2,3,1:T(8,128)(2,1)S(1)} %get-tuple-element.18), channel_id=1, source_target_pairs={{2,0},{4,2},{6,4},{8,6},{10,8},{12,10},{14,12},{16,14},{18,16},{20... | collective-permute-start | bytes 786440 | tf_op jit(solution)/shard_map/ppermute | solution.py:21
  48.0 5.2 %collective-permute-done.4 = bf16[64,1,16,128]{0,2,3,1:T(8,128)(2,1)S(1)} collective-permute-done((bf16[64,1,16,128]{0,2,3,1:T(8,128)(2,1)S(1)}, bf16[64,1,16,128]{0,2,3,1:T(8,128)(2,1)S(1)}, u32[]{:S(2)}, u32[]{:S(2)}) %collective-permute-start.4) | collective-permute-done | bytes 262176 | tf_op jit(solution)/shard_map/ppermute | solution.py:18
  61.5 4.0 %copy.113 = bf16[64,6,16,128]{3,0,2,1:T(8,128)(2,1)S(1)} copy(bf16[64,6,16,128]{0,2,3,1:T(8,128)(2,1)} %copy-done.4) | data formatting | bytes 3145728 | tf_op jit(solution)/shard_map/concatenate | solution.py:22
  72.0 4.3 %maximum_bitcast_fusion = bf16[64,6,18,1,130]{4,0,2,1,3:T(8,128)(2,1)} fusion(bf16[64,6,18,1]{3,0,2,1:T(8,128)(2,1)S(1)} %get-tuple-element.22, bf16[64,6,1,128]{3,0,2,1:T(8,128)(2,1)S(1)} %copy.114, bf16[64,6,16,128]{3,0,2,1:T(8,128)(2,1)S(1)} %copy.113, bf16[64,6,1,128]{3,0,2,1:T(8,128)(2,1)S(1)} %copy.112, bf16[64,6,18,1]{3,0,2,1:T(8,128)(2,1)S(1)} %get-tuple-element.21), kind=kLoop, calls=%fused_computation.37 | loop fusion | flops 8985600 | bytes 3594240 | tf_op jit(solution)/shard_map/broadcast_in_dim | solution.py:61
  76.3 6.2 %copy.134 = bf16[64,6,18,1,130]{0,4,2,1,3:T(8,128)(2,1)} copy(bf16[64,6,18,1,130]{4,0,2,1,3:T(8,128)(2,1)} %maximum_bitcast_fusion) | data formatting | bytes 3594240
  82.5 4.7 %pad.2.clone = bf16[64,6,18,1,136]{0,4,2,1,3:T(8,128)(2,1)} pad(bf16[64,6,18,1,130]{0,4,2,1,3:T(8,128)(2,1)} %copy.134, bf16[]{:T(256)} %constant.23), padding=0_0x0_0x0_0x0_0x0_6 | pad | bytes 3677186 | tf_op jit(solution)/shard_map/broadcast_in_dim | solution.py:61
  87.2 7.9 %reshape.16 = bf16[64,6,18,1,8,17]{0,5,4,2,1,3:T(8,128)(2,1)} reshape(bf16[64,6,18,1,136]{0,4,2,1,3:T(8,128)(2,1)} %pad.2.clone) | data formatting | bytes 3760128 | tf_op jit(solution)/shard_map/conv_general_dilated | solution.py:60
  98.4 17.6 %broadcast_select_fusion.1 = f32[4,16,8,17,64]{4,2,3,1,0:T(8,128)S(1)} fusion(pred[8,17]{0,1:T(8,128)(4,1)S(1)} %copy-done.35, bf16[64,64,3,3,3]{1,0,4,3,2:T(8,128)(2,1)S(1)} %copy-done, bf16[64,6,18,1,7,2]{0,4,5,2,1,3:T(8,128)(2,1)S(1)} %slice.462, bf16[64,6,18,1,8,17]{0,4,5,2,1,3:T(8,128)(2,1)S(1)} %copy.117), kind=kOutput, calls=%fused_computation.42 | convolution fusion | flops 1932046336 | bytes 4523144 | tf_op jit(solution)/shard_map/conv_general_dilated | solution.py:60
  118.4 6.0 %collective-permute-start.9 = (bf16[64,1,16,128]{0,2,3,1:T(8,128)(2,1)S(1)}, bf16[64,1,16,128]{0,2,3,1:T(8,128)(2,1)S(1)}, u32[]{:S(2)}, u32[]{:S(2)}) collective-permute-start(bf16[64,1,16,128]{0,2,3,1:T(8,128)(2,1)S(1)} %get-tuple-element.16), channel_id=1, source_target_pairs={{2,0},{4,2},{6,4},{8,6},{10,8},{12,10},{14,12},{16,14},{18,16},{20... | collective-permute-start | bytes 786440 | tf_op jit(solution)/shard_map/ppermute | solution.py:21
  125.9 5.4 %collective-permute-done.8 = bf16[64,1,16,128]{0,2,3,1:T(8,128)(2,1)S(1)} collective-permute-done((bf16[64,1,16,128]{0,2,3,1:T(8,128)(2,1)S(1)}, bf16[64,1,16,128]{0,2,3,1:T(8,128)(2,1)S(1)}, u32[]{:S(2)}, u32[]{:S(2)}) %collective-permute-start.8) | collective-permute-done | bytes 262176 | tf_op jit(solution)/shard_map/ppermute | solution.py:18
  139.3 4.0 %copy.120 = bf16[64,6,16,128]{3,0,2,1:T(8,128)(2,1)S(1)} copy(bf16[64,6,16,128]{0,2,3,1:T(8,128)(2,1)} %copy-done.3) | data formatting | bytes 3145728 | tf_op jit(solution)/shard_map/concatenate | solution.py:22
  144.5 4.0 %collective-permute-done.11 = bf16[64,6,1,128]{0,2,3,1:T(2,128)(2,1)S(1)} collective-permute-done((bf16[64,6,1,128]{0,2,3,1:T(2,128)(2,1)S(1)}, bf16[64,6,1,128]{0,2,3,1:T(2,128)(2,1)S(1)}, u32[]{:S(2)}, u32[]{:S(2)}) %collective-permute-start.11) | collective-permute-done | bytes 98336 | tf_op jit(solution)/shard_map/ppermute | solution.py:21
  149.8 4.3 %maximum_bitcast_fusion.1 = bf16[64,6,18,1,130]{4,0,2,1,3:T(8,128)(2,1)} fusion(bf16[64,6,18,1]{3,0,2,1:T(8,128)(2,1)S(1)} %get-tuple-element.20, bf16[64,6,1,128]{3,0,2,1:T(8,128)(2,1)S(1)} %copy.121, bf16[64,6,16,128]{3,0,2,1:T(8,128)(2,1)S(1)} %copy.120, bf16[64,6,1,128]{3,0,2,1:T(8,128)(2,1)S(1)} %copy.119, bf16[64,6,18,1]{3,0,2,1:T(8,128)(2,1)S(1)} %get-tuple-element.19), kind=kLoop, calls=%fused_computation.38 | loop fusion | flops 8985600 | bytes 3594240 | tf_op jit(solution)/shard_map/broadcast_in_dim | solution.py:61
  154.1 6.2 %copy.135 = bf16[64,6,18,1,130]{0,4,2,1,3:T(8,128)(2,1)} copy(bf16[64,6,18,1,130]{4,0,2,1,3:T(8,128)(2,1)} %maximum_bitcast_fusion.1) | data formatting | bytes 3594240
  160.4 4.7 %pad.4.clone = bf16[64,6,18,1,136]{0,4,2,1,3:T(8,128)(2,1)} pad(bf16[64,6,18,1,130]{0,4,2,1,3:T(8,128)(2,1)} %copy.135, bf16[]{:T(256)} %constant.23), padding=0_0x0_0x0_0x0_0x0_6 | pad | bytes 3677186 | tf_op jit(solution)/shard_map/broadcast_in_dim | solution.py:61
  165.0 7.9 %reshape.23 = bf16[64,6,18,1,8,17]{0,5,4,2,1,3:T(8,128)(2,1)} reshape(bf16[64,6,18,1,136]{0,4,2,1,3:T(8,128)(2,1)} %pad.4.clone) | data formatting | bytes 3760128 | tf_op jit(solution)/shard_map/conv_general_dilated | solution.py:60
  176.3 137.2 %broadcast_select_fusion = f32[4,16,8,17,6]{2,4,3,1,0:T(8,128)S(1)} fusion(pred[8,17]{0,1:T(8,128)(4,1)S(1)} %copy-done.35, bf16[64,6,18,1,7,2]{0,4,5,2,1,3:T(8,128)(2,1)S(1)} %slice.470, bf16[64,6,18,1,8,17]{0,4,5,2,1,3:T(8,128)(2,1)S(1)} %copy.124, bf16[6,64,3,3,3]{1,4,3,2,0:T(4,128)(2,1)S(1)} %copy-done.33), kind=kOutput, calls=%fused_computation.41 | convolution fusion | flops 186842112 | bytes 2303368 | tf_op jit(solution)/shard_map/conv_general_dilated | solution.py:60
  322.2 4.0 %copy.126 = f32[4,16,8,17,6]{3,2,1,4,0:T(8,128)S(1)} copy(f32[4,16,8,17,6]{2,4,3,1,0:T(8,128)} %copy-done.5) | data formatting | bytes 417792 | tf_op jit(solution)/shard_map/conv_general_dilated | solution.py:60
  327.0 6.0 %collective-permute-start.13 = (bf16[6,3,16,128]{3,2,0,1:T(8,128)(2,1)S(1)}, bf16[6,3,16,128]{3,2,0,1:T(8,128)(2,1)S(1)}, u32[]{:S(2)}, u32[]{:S(2)}) collective-permute-start(bf16[6,3,16,128]{3,2,0,1:T(8,128)(2,1)S(1)} %get-tuple-element.63), channel_id=1, source_target_pairs={{2,0},{4,2},{6,4},{8,6},{10,8},{12,10},{14,12},{16,14},{18,16},{20... | collective-permute-start | bytes 221192 | tf_op jit(solution)/shard_map/ppermute | solution.py:21
  339.3 5.5 %collective-permute-done.15 = bf16[6,10,3,128]{3,2,0,1:T(4,128)(2,1)S(1)} collective-permute-done((bf16[6,10,3,128]{3,2,0,1:T(4,128)(2,1)S(1)}, bf16[6,10,3,128]{3,2,0,1:T(4,128)(2,1)S(1)}, u32[]{:S(2)}, u32[]{:S(2)}) %collective-permute-start.15) | collective-permute-done | bytes 46112 | tf_op jit(solution)/shard_map/ppermute | solution.py:21
  (170 shorter events, 68.6 us)
Async XLA Ops:
  0.6 97.8 %copy-start = (bf16[64,64,3,3,3]{1,0,4,3,2:T(8,128)(2,1)S(1)}, bf16[64,64,3,3,3]{1,0,4,3,2:T(8,128)(2,1)}, u32[]{:S(2)}) copy-start(bf16[64,64,3,3,3]{1,0,4,3,2:T(8,128)(2,1)} %param.6) | copy-start | bytes 663556
  1.7 9.8 %collective-permute-start.1 = (f32[3,3,16,128]{3,2,0,1:T(8,128)S(1)}, f32[3,3,16,128]{3,2,0,1:T(8,128)S(1)}, u32[]{:S(2)}, u32[]{:S(2)}) collective-permute-start(f32[3,3,16,128]{3,2,0,1:T(8,128)S(1)} %copy.144), channel_id=1, source_target_pairs={{0,2},{2,4},{4,6},{6,8},{8,10},{10,12},{12,14},{14,16},{16,18},{18... | collective-permute-start | bytes 221192 | tf_op jit(solution)/shard_map/ppermute | solution.py:18
  1.8 10.7 %collective-permute-start = (f32[3,3,16,128]{3,2,0,1:T(8,128)S(1)}, f32[3,3,16,128]{3,2,0,1:T(8,128)S(1)}, u32[]{:S(2)}, u32[]{:S(2)}) collective-permute-start(f32[3,3,16,128]{3,2,0,1:T(8,128)S(1)} %copy.145), channel_id=1, source_target_pairs={{2,0},{4,2},{6,4},{8,6},{10,8},{12,10},{14,12},{16,14},{18,16},{20... | collective-permute-start | bytes 221192 | tf_op jit(solution)/shard_map/ppermute | solution.py:21
  12.5 7.4 %collective-permute-start.3 = (f32[3,10,3,128]{3,2,0,1:T(4,128)S(1)}, f32[3,10,3,128]{3,2,0,1:T(4,128)S(1)}, u32[]{:S(2)}, u32[]{:S(2)}) collective-permute-start(f32[3,10,3,128]{3,2,0,1:T(4,128)S(1)} %get-tuple-element.28), channel_id=1, source_target_pairs={{0,1},{2,3},{4,5},{6,7},{8,9},{10,11},{12,13},{14,15},{16,17},{18,... | collective-permute-start | bytes 138248 | tf_op jit(solution)/shard_map/ppermute | solution.py:18
  16.9 7.6 %collective-permute-start.2 = (f32[3,10,3,128]{3,2,0,1:T(4,128)S(1)}, f32[3,10,3,128]{3,2,0,1:T(4,128)S(1)}, u32[]{:S(2)}, u32[]{:S(2)}) collective-permute-start(f32[3,10,3,128]{3,2,0,1:T(4,128)S(1)} %get-tuple-element.29), channel_id=1, source_target_pairs={{1,0},{3,2},{5,4},{7,6},{9,8},{11,10},{13,12},{15,14},{17,16},{19,... | collective-permute-start | bytes 138248 | tf_op jit(solution)/shard_map/ppermute | solution.py:21
  40.3 12.9 %collective-permute-start.4 = (bf16[64,1,16,128]{0,2,3,1:T(8,128)(2,1)S(1)}, bf16[64,1,16,128]{0,2,3,1:T(8,128)(2,1)S(1)}, u32[]{:S(2)}, u32[]{:S(2)}) collective-permute-start(bf16[64,1,16,128]{0,2,3,1:T(8,128)(2,1)S(1)} %get-tuple-element.17), channel_id=1, source_target_pairs={{0,2},{2,4},{4,6},{6,8},{8,10},{10,12},{12,14},{14,16},{16,18},{18... | collective-permute-start | bytes 786440 | tf_op jit(solution)/shard_map/ppermute | solution.py:18
  40.4 12.9 %collective-permute-start.5 = (bf16[64,1,16,128]{0,2,3,1:T(8,128)(2,1)S(1)}, bf16[64,1,16,128]{0,2,3,1:T(8,128)(2,1)S(1)}, u32[]{:S(2)}, u32[]{:S(2)}) collective-permute-start(bf16[64,1,16,128]{0,2,3,1:T(8,128)(2,1)S(1)} %get-tuple-element.18), channel_id=1, source_target_pairs={{2,0},{4,2},{6,4},{8,6},{10,8},{12,10},{14,12},{16,14},{18,16},{20... | collective-permute-start | bytes 786440 | tf_op jit(solution)/shard_map/ppermute | solution.py:21
  57.1 8.4 %collective-permute-start.6 = (bf16[64,6,1,128]{0,2,3,1:T(2,128)(2,1)}, bf16[64,6,1,128]{0,2,3,1:T(2,128)(2,1)}, u32[]{:S(2)}, u32[]{:S(2)}) collective-permute-start(bf16[64,6,1,128]{0,2,3,1:T(2,128)(2,1)} %get-tuple-element.13), channel_id=1, source_target_pairs={{0,1},{2,3},{4,5},{6,7},{8,9},{10,11},{12,13},{14,15},{16,17},{18,... | collective-permute-start | bytes 294920 | tf_op jit(solution)/shard_map/ppermute | solution.py:18
  59.5 11.2 %collective-permute-start.7 = (bf16[64,6,1,128]{0,2,3,1:T(2,128)(2,1)S(1)}, bf16[64,6,1,128]{0,2,3,1:T(2,128)(2,1)S(1)}, u32[]{:S(2)}, u32[]{:S(2)}) collective-permute-start(bf16[64,6,1,128]{0,2,3,1:T(2,128)(2,1)S(1)} %get-tuple-element.14), channel_id=1, source_target_pairs={{1,0},{3,2},{5,4},{7,6},{9,8},{11,10},{13,12},{15,14},{17,16},{19,... | collective-permute-start | bytes 294920 | tf_op jit(solution)/shard_map/ppermute | solution.py:21
  118.3 12.9 %collective-permute-start.8 = (bf16[64,1,16,128]{0,2,3,1:T(8,128)(2,1)S(1)}, bf16[64,1,16,128]{0,2,3,1:T(8,128)(2,1)S(1)}, u32[]{:S(2)}, u32[]{:S(2)}) collective-permute-start(bf16[64,1,16,128]{0,2,3,1:T(8,128)(2,1)S(1)} %get-tuple-element.15), channel_id=1, source_target_pairs={{0,2},{2,4},{4,6},{6,8},{8,10},{10,12},{12,14},{14,16},{16,18},{18... | collective-permute-start | bytes 786440 | tf_op jit(solution)/shard_map/ppermute | solution.py:18
  118.4 12.8 %collective-permute-start.9 = (bf16[64,1,16,128]{0,2,3,1:T(8,128)(2,1)S(1)}, bf16[64,1,16,128]{0,2,3,1:T(8,128)(2,1)S(1)}, u32[]{:S(2)}, u32[]{:S(2)}) collective-permute-start(bf16[64,1,16,128]{0,2,3,1:T(8,128)(2,1)S(1)} %get-tuple-element.16), channel_id=1, source_target_pairs={{2,0},{4,2},{6,4},{8,6},{10,8},{12,10},{14,12},{16,14},{18,16},{20... | collective-permute-start | bytes 786440 | tf_op jit(solution)/shard_map/ppermute | solution.py:21
  134.4 8.9 %collective-permute-start.10 = (bf16[64,6,1,128]{0,2,3,1:T(2,128)(2,1)S(1)}, bf16[64,6,1,128]{0,2,3,1:T(2,128)(2,1)}, u32[]{:S(2)}, u32[]{:S(2)}) collective-permute-start(bf16[64,6,1,128]{0,2,3,1:T(2,128)(2,1)S(1)} %get-tuple-element.11), channel_id=1, source_target_pairs={{0,1},{2,3},{4,5},{6,7},{8,9},{10,11},{12,13},{14,15},{16,17},{18,... | collective-permute-start | bytes 294920 | tf_op jit(solution)/shard_map/ppermute | solution.py:18
  137.3 11.2 %collective-permute-start.11 = (bf16[64,6,1,128]{0,2,3,1:T(2,128)(2,1)S(1)}, bf16[64,6,1,128]{0,2,3,1:T(2,128)(2,1)S(1)}, u32[]{:S(2)}, u32[]{:S(2)}) collective-permute-start(bf16[64,6,1,128]{0,2,3,1:T(2,128)(2,1)S(1)} %get-tuple-element.12), channel_id=1, source_target_pairs={{1,0},{3,2},{5,4},{7,6},{9,8},{11,10},{13,12},{15,14},{17,16},{19,... | collective-permute-start | bytes 294920 | tf_op jit(solution)/shard_map/ppermute | solution.py:21
  326.2 19.0 %copy-start.7 = (f32[3,7,16,128]{3,2,0,1:T(8,128)S(1)}, f32[3,7,16,128]{3,2,0,1:T(8,128)}, u32[]{:S(2)}) copy-start(f32[3,7,16,128]{3,2,0,1:T(8,128)} %copy-done.6) | copy-start | bytes 516100
  326.7 18.6 %copy-start.8 = (f32[3,4,16,127]{3,2,1,0:T(8,128)S(1)}, f32[3,4,16,127]{3,2,1,0:T(8,128)}, u32[]{:S(2)}) copy-start(f32[3,4,16,127]{3,2,1,0:T(8,128)} %get-tuple-element.38) | copy-start | bytes 292612
  326.7 18.6 %copy-start.9 = (f32[3,4,16,127]{3,2,1,0:T(8,128)S(1)}, f32[3,4,16,127]{3,2,1,0:T(8,128)}, u32[]{:S(2)}) copy-start(f32[3,4,16,127]{3,2,1,0:T(8,128)} %get-tuple-element.39) | copy-start | bytes 292612
  326.7 18.6 %copy-start.10 = (f32[3,4,16,1]{3,2,1,0:T(8,128)S(1)}, f32[3,4,16,1]{3,2,1,0:T(8,128)}, u32[]{:S(2)}) copy-start(f32[3,4,16,1]{3,2,1,0:T(8,128)} %get-tuple-element.40) | copy-start | bytes 2308
  326.7 18.6 %copy-start.11 = (f32[3,4,16,1]{3,2,1,0:T(8,128)S(1)}, f32[3,4,16,1]{3,2,1,0:T(8,128)}, u32[]{:S(2)}) copy-start(f32[3,4,16,1]{3,2,1,0:T(8,128)} %get-tuple-element.41) | copy-start | bytes 2308
  326.7 18.6 %copy-start.12 = (f32[3,4,16,126]{3,2,1,0:T(8,128)S(1)}, f32[3,4,16,126]{3,2,1,0:T(8,128)}, u32[]{:S(2)}) copy-start(f32[3,4,16,126]{3,2,1,0:T(8,128)} %get-tuple-element.42) | copy-start | bytes 290308
  326.7 18.6 %copy-start.13 = (f32[3,4,16,126]{3,2,1,0:T(8,128)S(1)}, f32[3,4,16,126]{3,2,1,0:T(8,128)}, u32[]{:S(2)}) copy-start(f32[3,4,16,126]{3,2,1,0:T(8,128)} %get-tuple-element.43) | copy-start | bytes 290308
  327.0 8.2 %collective-permute-start.12 = (bf16[6,3,16,128]{3,2,0,1:T(8,128)(2,1)S(1)}, bf16[6,3,16,128]{3,2,0,1:T(8,128)(2,1)S(1)}, u32[]{:S(2)}, u32[]{:S(2)}) collective-permute-start(bf16[6,3,16,128]{3,2,0,1:T(8,128)(2,1)S(1)} %get-tuple-element.62), channel_id=1, source_target_pairs={{0,2},{2,4},{4,6},{6,8},{8,10},{10,12},{12,14},{14,16},{16,18},{18... | collective-permute-start | bytes 221192 | tf_op jit(solution)/shard_map/ppermute | solution.py:18
  327.0 8.1 %collective-permute-start.13 = (bf16[6,3,16,128]{3,2,0,1:T(8,128)(2,1)S(1)}, bf16[6,3,16,128]{3,2,0,1:T(8,128)(2,1)S(1)}, u32[]{:S(2)}, u32[]{:S(2)}) collective-permute-start(bf16[6,3,16,128]{3,2,0,1:T(8,128)(2,1)S(1)} %get-tuple-element.63), channel_id=1, source_target_pairs={{2,0},{4,2},{6,4},{8,6},{10,8},{12,10},{14,12},{16,14},{18,16},{20... | collective-permute-start | bytes 221192 | tf_op jit(solution)/shard_map/ppermute | solution.py:21
  335.2 4.1 %collective-permute-start.14 = (bf16[6,10,3,128]{3,2,0,1:T(4,128)(2,1)S(1)}, bf16[6,10,3,128]{3,2,0,1:T(4,128)(2,1)S(1)}, u32[]{:S(2)}, u32[]{:S(2)}) collective-permute-start(bf16[6,10,3,128]{3,2,0,1:T(4,128)(2,1)S(1)} %get-tuple-element.26), channel_id=1, source_target_pairs={{0,1},{2,3},{4,5},{6,7},{8,9},{10,11},{12,13},{14,15},{16,17},{18,... | collective-permute-start | bytes 138248 | tf_op jit(solution)/shard_map/ppermute | solution.py:18
  337.2 7.6 %collective-permute-start.15 = (bf16[6,10,3,128]{3,2,0,1:T(4,128)(2,1)S(1)}, bf16[6,10,3,128]{3,2,0,1:T(4,128)(2,1)S(1)}, u32[]{:S(2)}, u32[]{:S(2)}) collective-permute-start(bf16[6,10,3,128]{3,2,0,1:T(4,128)(2,1)S(1)} %get-tuple-element.27), channel_id=1, source_target_pairs={{1,0},{3,2},{5,4},{7,6},{9,8},{11,10},{13,12},{15,14},{17,16},{19,... | collective-permute-start | bytes 138248 | tf_op jit(solution)/shard_map/ppermute | solution.py:21
  (28 other events, 398.5 us)
where the time goes:
time: 351 us; the launch traced here: 347 us
  matrix products  163 us (46%)
  local copies, waits for them, and re-layouts  91.5 us (26%)
  starting transfers between devices  43 us (12%)
  waiting for transfers between devices  32.6 us (9%)
  other arithmetic  14.6 us (4%)
    conv_general_dilated x3, matrix products, conv_valid(): lax.conv_general_dilated(wide[None], kernel, (1, 1, 1), 'VALID', dimensio...  163 us
    conv_general_dilated x20, local copies, waits for them, and re-layouts, conv_valid(): lax.conv_general_dilated(wide[None], kernel, (1, 1, 1), 'VALID', dimensio...  36.1 us
    ppermute x8, starting transfers between devices, padded(): lax.ppermute(lax.slice_in_dim(block, 0, width, axis=dim), axis, backward)  31 us
    unnamed x80, local copies, waits for them, and re-layouts  20.4 us
    ppermute x8, waiting for transfers between devices, padded(): lax.ppermute(lax.slice_in_dim(block, 0, width, axis=dim), axis, backward)  18 us
    ppermute x8, waiting for transfers between devices, padded(): lax.ppermute(lax.slice_in_dim(block, block.shape[dim] - width, None, axis...  14.5 us
    ppermute x8, starting transfers between devices, padded(): lax.ppermute(lax.slice_in_dim(block, block.shape[dim] - width, None, axis...  12 us
    broadcast_in_dim x3, local copies, waits for them, and re-layouts, conv_valid(): wide[None]  9.42 us
  transfers between devices with their start and end apart: 16, of which 9 were waited for; matrix products, arithmetic and copies ran while one was open for 5% of the time, Pallas kernels for 0%

commit v1 on v0

v1 whole, which is shorter than its diff:
```python
import functools
import math

import jax
import jax.numpy as jnp
from jax import lax
from jax.experimental import pallas as pl
from jax.experimental.pallas import tpu as pltpu
from jax.sharding import PartitionSpec as P

MESH = pl.DeviceIdType.MESH
F32 = jnp.float32
BF16 = jnp.bfloat16

A1 = (0.75, -0.15, 1.0 / 60.0)
A2 = (1.5, -0.15, 1.0 / 90.0)
CENTER = -49.0 / 18.0
G0 = math.sqrt(2.0 / math.pi)
G1 = G0 * 0.044715

ORDER = (0, 4, 3, 1, 5, 2)
URO = 20 * 16


def gelu(s):
    half = 0.5 * s
    return half + half * jnp.tanh(s * (G0 + G1 * (s * s)))


def spin(a, k):
    return pltpu.roll(a, k % 128, 1)


def band(w0, w1, w2):
    zero = jnp.zeros_like(w0)
    cat = lambda a, b: jnp.concatenate([a, b], axis=1)
    return cat(w0, w1), cat(w2, zero), cat(zero, w0), cat(w1, w2)


def kernel(
    vel_hbm, wi_hbm, wm_hbm, wo_hbm, ten_ref, str_ref,
    v, hx, hy, ysend, uf, u16, wi_raw, wm_raw, wo_raw, wt0, wt1, wi, wp, wof, wo, h1, h2, q, ve, s, s16, ys16, sx, sy, se,
    load_sem, send_a, recv_a, send_b, recv_b,
):
    n = 128
    gx = lax.axis_index("gx")
    gy = lax.axis_index("gy")
    lo = lax.rem(gx + n - 1, n)
    hi = lax.rem(gx + 1, n)
    oy = 1 - gy
    peers = ((lo, gy), (hi, gy), (gx, oy), (lo, oy), (hi, oy))
    opposite = (1, 0, 2, 4, 3)

    barrier = pltpu.get_barrier_semaphore()
    for peer in peers:
        pl.semaphore_signal(barrier, inc=1, device_id=peer, device_id_type=MESH)
    loads = [
        pltpu.make_async_copy(vel_hbm, v.at[pl.ds(0, 192)], load_sem.at[0]),
        pltpu.make_async_copy(wi_hbm, wi_raw, load_sem.at[1]),
        pltpu.make_async_copy(wm_hbm, wm_raw, load_sem.at[2]),
        pltpu.make_async_copy(wo_hbm, wo_raw, load_sem.at[3]),
    ]
    for load in loads:
        load.start()
    v[pl.ds(192, 64), :] = jnp.zeros((64, 128), F32)
    loads[0].wait()
    near = 13 * (1 - gy)
    for r in range(3):
        ysend[r] = v[pl.ds(near + r, 16, stride=16), :]
    pl.semaphore_wait(barrier, 5)

    v3 = v.at[pl.ds(0, 192)].reshape(3, 64, 128)
    sends = []
    for k in range(5):
        if k == 0:
            src, dst = v3.at[:, pl.ds(0, 48), :], hx.at[opposite[k]]
        elif k == 1:
            src, dst = v3.at[:, pl.ds(16, 48), :], hx.at[opposite[k]]
        else:
            src, dst = ysend, hy.at[opposite[k] - 2]
        sends.append(
            pltpu.make_async_remote_copy(
                src_ref=src, dst_ref=dst, send_sem=send_a.at[k], recv_sem=recv_a.at[opposite[k]],
                device_id=peers[k], device_id_type=MESH,
            )
        )
        sends[-1].start()

    @pl.loop(0, 10)
    def _(i):
        uf[pl.ds(i * URO, URO), :] = jnp.zeros((URO, 128), F32)

    def patch(field, x, c):
        for dz in range(3):
            start = x * URO + (2 * gy + 1) * 16 + dz * 3 + c
            uf[pl.ds(start, 16, stride=16), :] = spin(field, 1 - dz)

    for c in range(3):
        for x in range(4):
            patch(v[pl.ds((c * 4 + x) * 16, 16), :], x + 3, c)

    loads[1].wait()
    wt0[...] = jnp.zeros_like(wt0)
    wt1[...] = jnp.zeros_like(wt1)
    for c in range(3):
        for dx in range(3):
            for dy in range(3):
                w = wi_raw[c, dx, dy].astype(F32)
                wide = jnp.concatenate([w, jnp.zeros_like(w)], axis=1)
                row = dx * 48 + dy * 16 + c
                wt0[pl.ds(row, 3, stride=3), :] = wide
                wt1[pl.ds(row + 48, 3, stride=3), :] = spin(wide, 64)
    wi[...] = (wt0[...] + wt1[...]).T[:, :192].astype(BF16)

    loads[2].wait()
    for dy in range(3):
        for dz in range(3):
            a, b, c, d = band(wm_raw[0, dy, dz], wm_raw[1, dy, dz], wm_raw[2, dy, dz])
            wp[pl.ds(dz * 128, 64), pl.ds(dy * 256, 128)] = a
            wp[pl.ds(dz * 128, 64), pl.ds(dy * 256 + 128, 128)] = b
            wp[pl.ds(dz * 128 + 64, 64), pl.ds(dy * 256, 128)] = c
            wp[pl.ds(dz * 128 + 64, 64), pl.ds(dy * 256 + 128, 128)] = d

    loads[3].wait()
    wof[...] = jnp.zeros_like(wof)
    for k in range(6):
        for dy in range(3):
            a, b, c, d = band(*(wo_raw[ORDER[k], dx, dy].astype(F32) for dx in range(3)))
            for x in range(4):
                first, second = ((a, b), (c, d))[x % 2]
                rows = pl.ds(dy * 72 + k * 4 + x, 3, stride=24)
                wof[x // 2, rows, :] = first
                wof[x // 2 + 1, rows, :] = second
    for m in range(3):
        wo[:, pl.ds(m * 128, 128)] = wof[m].astype(BF16)

    h1[0] = jnp.zeros((512, 128), BF16)
    h1[19] = jnp.zeros((512, 128), BF16)
    for dy in range(3):
        q[dy, 0] = jnp.zeros((24, 128), F32)
        q[dy, 19] = jnp.zeros((24, 128), F32)

    for k in range(5):
        sends[k].wait_recv()

    for c in range(3):
        for x in range(3):
            patch(hx[0, c, pl.ds(x * 16, 16), :], x, c)
            patch(hx[1, c, pl.ds(x * 16, 16), :], x + 7, c)
    far = jnp.where(gy == 0, 17, 0)
    for r in range(3):
        for side, x_from, x_to, count in ((0, 0, 3, 4), (1, 1, 0, 3), (2, 0, 7, 3)):
            row = hy[side, r]
            for dz in range(3):
                turned = spin(row, 1 - dz)
                for c in range(3):
                    start = x_to * URO + (far + r) * 16 + dz * 3 + c
                    uf[pl.ds(start, count, stride=URO), :] = turned[c * 4 + x_from:c * 4 + x_from + count]

    @pl.loop(0, 10)
    def _(i):
        u16[pl.ds(i * URO, URO), :] = uf[pl.ds(i * URO, URO), :].astype(BF16)

    @pl.loop(0, 9)
    def _(t):
        j = t * 2
        for p in range(4):
            def rows(dj):
                return jnp.concatenate(
                    [u16[pl.ds((2 * p + i) * URO + (j + dj) * 16, 48), :] for i in range(4)], axis=0
                )
            out = gelu(jnp.dot(wi[...], jnp.concatenate([rows(0), rows(1)], axis=1), preferred_element_type=F32))
            out = out.astype(BF16)
            h1[j + 1, pl.ds(p * 128, 128), :] = out[:, :128]
            h1[j + 2, pl.ds(p * 128, 128), :] = out[:, 128:]

    @pl.loop(0, 9)
    def _(t):
        j = t * 2
        for p in range(3):
            def rows(dj):
                return jnp.concatenate(
                    [h1[j + dj + dy, pl.ds(p * 128, 256), :] for dy in range(3)], axis=0
                )
            part = jnp.dot(wp[...], jnp.concatenate([rows(0), rows(1)], axis=1), preferred_element_type=F32)
            for dj in range(2):
                half = part[:, dj * 128:dj * 128 + 128]
                out = gelu(spin(half[0:128], 1) + half[128:256] + spin(half[256:384], -1))
                h2[j + dj, pl.ds(p * 128, 128), :] = out.astype(BF16)

    @pl.loop(0, 9)
    def _(t):
        j = t * 2
        part = jnp.dot(wo[...], jnp.concatenate([h2[j], h2[j + 1]], axis=1), preferred_element_type=F32)
        for dj in range(2):
            half = part[:, dj * 128:dj * 128 + 128]
            for dy in range(3):
                at = dy * 72
                q[dy, j + dj + 1] = (
                    spin(half[at:at + 24], 1) + half[at + 24:at + 48] + spin(half[at + 48:at + 72], -1)
                )

    @pl.loop(0, 16)
    def _(y):
        j = y + 2 * gy
        s[pl.ds(y, 24, stride=16), :] = q[0, j] + q[1, j + 1] + q[2, j + 2]

    for k in range(3):
        s16[k] = s[pl.ds(k * 64, 64), :].astype(BF16)
    for r in range(3):
        ys16[r] = s[pl.ds(128 + near + r, 16, stride=16), :].astype(BF16)
    last = []
    for k in range(3):
        if k == 0:
            src, dst = s16.at[:, pl.ds(0, 48), :], sx.at[1]
        elif k == 1:
            src, dst = s16.at[:, pl.ds(16, 48), :], sx.at[0]
        else:
            src, dst = ys16, sy
        last.append(
            pltpu.make_async_remote_copy(
                src_ref=src, dst_ref=dst, send_sem=send_b.at[k], recv_sem=recv_b.at[opposite[k]],
                device_id=peers[k], device_id_type=MESH,
            )
        )
        last[-1].start()

    low_side = gy == 1

    def edge(ext, halo, count):
        for r in range(3):
            row = halo(r)
            ext[pl.ds(24 + r, count, stride=32), :] = jnp.where(low_side, 0.0, row)
            ext[pl.ds(5 + r, count, stride=32), :] = jnp.where(low_side, row, 0.0)

    def x_plane(c, x):
        if x < 0:
            return hx[0, c, pl.ds((x + 3) * 16, 16), :]
        if x > 3:
            return hx[1, c, pl.ds((x - 4) * 16, 16), :]
        return v[pl.ds((c * 4 + x) * 16, 16), :]

    for i in range(12):
        ve[pl.ds(i * 32 + 8, 16), :] = v[pl.ds(i * 16, 16), :]
    edge(ve, lambda r: hy[0, r, pl.ds(0, 12), :], 12)
    for c in range(3):
        for x in range(4):
            mid = x_plane(c, x)
            base = (c * 4 + x) * 32 + 8
            d1 = [0.0, 0.0, 0.0]
            d2 = (3.0 * CENTER) * mid
            for k in range(3):
                pairs = (
                    (x_plane(c, x + k + 1), x_plane(c, x - k - 1)),
                    (ve[pl.ds(base + k + 1, 16), :], ve[pl.ds(base - k - 1, 16), :]),
                    (spin(mid, -k - 1), spin(mid, k + 1)),
                )
                for a, (up, down) in enumerate(pairs):
                    d1[a] = d1[a] + A1[k] * (up - down)
                    d2 = d2 + A2[k] * (up + down)
            advect = x_plane(0, x) * d1[0] + x_plane(1, x) * d1[1] + x_plane(2, x) * d1[2]
            ten_ref[pl.ds((c * 4 + x) * 16, 16), :] = 0.2 * d2 - advect
    for k in range(6):
        str_ref[pl.ds(ORDER[k] * 64, 64), :] = s[pl.ds(k * 64, 64), :]
    for i in range(12):
        se[pl.ds(i * 32 + 8, 16), :] = s[pl.ds(128 + i * 16, 16), :]

    for k in range(3):
        last[k].wait_recv()

    def s_plane(k, x):
        if x < 0:
            return sx[0, k, pl.ds((x + 3) * 16, 16), :].astype(F32)
        if x > 3:
            return sx[1, k, pl.ds((x - 4) * 16, 16), :].astype(F32)
        return s[pl.ds((k * 4 + x) * 16, 16), :]

    edge(se, lambda r: sy[r].astype(F32)[:12], 12)
    for c, (along_x, along_y, along_z) in enumerate(((0, 0, 1), (2, 1, 4), (1, 2, 5))):
        for x in range(4):
            base = (along_y * 4 + x) * 32 + 8
            mid = s[pl.ds((along_z * 4 + x) * 16, 16), :]
            total = ten_ref[pl.ds((c * 4 + x) * 16, 16), :]
            for k in range(3):
                total = total - A1[k] * (
                    (s_plane(along_x, x + k + 1) - s_plane(along_x, x - k - 1))
                    + (se[pl.ds(base + k + 1, 16), :] - se[pl.ds(base - k - 1, 16), :])
                    + (spin(mid, -k - 1) - spin(mid, k + 1))
                )
            ten_ref[pl.ds((c * 4 + x) * 16, 16), :] = total

    for send in sends + last:
        send.wait_send()


def shards(velocity, kernel_in, kernel_mid, kernel_out):
    anywhere = pl.BlockSpec(memory_space=pl.ANY)
    whole = pl.BlockSpec(memory_space=pltpu.VMEM)
    tendency, stress = pl.pallas_call(
        kernel,
        out_shape=(jax.ShapeDtypeStruct((192, 128), F32), jax.ShapeDtypeStruct((384, 128), F32)),
        in_specs=[anywhere] * 4,
        out_specs=(whole, whole),
        scratch_shapes=[
            pltpu.VMEM((256, 128), F32),
            pltpu.VMEM((2, 3, 48, 128), F32),
            pltpu.VMEM((3, 3, 16, 128), F32),
            pltpu.VMEM((3, 16, 128), F32),
            pltpu.VMEM((10 * URO, 128), F32),
            pltpu.VMEM((10 * URO, 128), BF16),
            pltpu.VMEM((3, 3, 3, 3, 64), BF16),
            pltpu.VMEM((3, 3, 3, 64, 64), BF16),
            pltpu.VMEM((6, 3, 3, 3, 64), BF16),
            pltpu.VMEM((256, 128), F32),
            pltpu.VMEM((256, 128), F32),
            pltpu.VMEM((128, 192), BF16),
            pltpu.VMEM((384, 768), BF16),
            pltpu.VMEM((3, 216, 128), F32),
            pltpu.VMEM((216, 384), BF16),
            pltpu.VMEM((20, 512, 128), BF16),
            pltpu.VMEM((18, 384, 128), BF16),
            pltpu.VMEM((3, 20, 24, 128), F32),
            pltpu.VMEM((12 * 32, 128), F32),
            pltpu.VMEM((384, 128), F32),
            pltpu.VMEM((3, 64, 128), BF16),
            pltpu.VMEM((3, 16, 128), BF16),
            pltpu.VMEM((2, 3, 48, 128), BF16),
            pltpu.VMEM((3, 16, 128), BF16),
            pltpu.VMEM((12 * 32, 128), F32),
            pltpu.SemaphoreType.DMA((4,)),
            pltpu.SemaphoreType.DMA((5,)),
            pltpu.SemaphoreType.DMA((5,)),
            pltpu.SemaphoreType.DMA((3,)),
            pltpu.SemaphoreType.DMA((3,)),
        ],
        compiler_params=pltpu.CompilerParams(
            collective_id=0, has_side_effects=True, vmem_limit_bytes=48 * 1024 * 1024
        ),
    )(
        velocity.reshape(192, 128),
        jnp.transpose(kernel_in, (1, 2, 3, 4, 0)),
        jnp.transpose(kernel_mid, (2, 3, 4, 0, 1)),
        jnp.transpose(kernel_out, (0, 2, 3, 4, 1)),
    )
    return tendency.reshape(3, 4, 16, 128), stress.reshape(6, 4, 16, 128)


def solution(mesh):
    placed = (P(None, "gx", "gy", None), P(), P(), P())
    return jax.shard_map(
        shards,
        mesh=mesh,
        in_specs=placed,
        out_specs=(P(None, "gx", "gy", None), P(None, "gx", "gy", None)),
        check_vma=False,
    )
```

time: 351 us -> 38.5 us (0.11)
  matrix products: 163 us -> 0 us
  local copies, waits for them, and re-layouts: 91.5 us -> 4.78 us
  starting transfers between devices: 43 us -> 0 us
  waiting for transfers between devices: 32.6 us -> 0 us
  Pallas kernels: 0 us -> 32.5 us
  other arithmetic: 14.6 us -> 0 us
    conv_general_dilated x3 -> x0, matrix products: 163 us -> none  [conv_valid(): lax.conv_general_dilated(wide[None], kernel, (1, 1, 1), 'VALID', dimensio...]
    ppermute x16 -> x0, starting transfers between devices: 43 us -> none  [the longest x8 31 us: padded(): lax.ppermute(lax.slice_in_dim(block, 0, width, axis=dim), axis, backward)]
    conv_general_dilated x20 -> x0, local copies, waits for them, and re-layouts: 36.1 us -> none  [conv_valid(): lax.conv_general_dilated(wide[None], kernel, (1, 1, 1), 'VALID', dimensio...]
    ppermute x16 -> x0, waiting for transfers between devices: 32.6 us -> none  [the longest x8 18 us: padded(): lax.ppermute(lax.slice_in_dim(block, 0, width, axis=dim), axis, backward)]
    pallas_call x0 -> x1, Pallas kernels: none -> 32.5 us  [shards(): pl.pallas_call(kernel, out_shape=(jax.ShapeDtypeStruct((192, 128), F32),...]
    unnamed x80 -> x10, local copies, waits for them, and re-layouts: 20.4 us -> 4.78 us
    slice x26 -> x0, local copies, waits for them, and re-layouts: 13.9 us -> none  [the longest x6 5.38 us: first_span(): jnp.roll(field, -step, 3) - jnp.roll(field, step, 3)]
    broadcast_in_dim x3 -> x0, local copies, waits for them, and re-layouts: 9.42 us -> none  [conv_valid(): wide[None]]
  transfers between devices with their start and end apart: 16 -> 0, of which waited for: 9 -> 0; matrix products, arithmetic and copies ran while one was open for 5% -> 0% of each run, Pallas kernels for 0% -> 0%
where the time goes in v1:
time: 38.5 us; the launch traced here: 37.9 us
  Pallas kernels  32.5 us (84%)
  local copies, waits for them, and re-layouts  4.78 us (12%)
  between operations  0.65 us (2%)
    pallas_call x1, Pallas kernels, shards(): pl.pallas_call(kernel, out_shape=(jax.ShapeDtypeStruct((192, 128), F32),...  32.5 us
    unnamed x10, local copies, waits for them, and re-layouts  4.78 us

profile of v1, /device:TPU:2, one launch (start us, length us, event | category | flops | bytes accessed | tf_op | source)
XLA Modules:
  0.0 37.9 jit_solution(9243791461217324366)
XLA Ops:
  0.6 0.0 copy-start
  0.6 1.0 %copy-done = bf16[64,64,3,3,3]{1,0,4,3,2:T(8,128)(2,1)S(1)} copy-done((bf16[64,64,3,3,3]{1,0,4,3,2:T(8,128)(2,1)S(1)}, bf16[64,64,3,3,3]{1,0,4,3,2:T(8,128)(2,1)}, u32[]{:S(2)}) %copy-start) | copy-done | bytes 221208
  1.6 0.0 copy-start.1
  1.6 0.9 %copy-done.1 = f32[3,4,16,128]{3,2,1,0:T(8,128)S(1)} copy-done((f32[3,4,16,128]{3,2,1,0:T(8,128)S(1)}, f32[3,4,16,128]{3,2,1,0:T(8,128)}, u32[]{:S(2)}) %copy-start.1) | copy-done | bytes 98328
  2.5 0.0 copy-start.2
  2.5 0.8 %copy-done.2 = bf16[6,64,3,3,3]{1,4,3,2,0:T(4,128)(2,1)S(1)} copy-done((bf16[6,64,3,3,3]{1,4,3,2,0:T(4,128)(2,1)S(1)}, bf16[6,64,3,3,3]{1,4,3,2,0:T(4,128)(2,1)}, u32[]{:S(2)}) %copy-start.2) | copy-done | bytes 20760
  3.4 0.0 copy-start.3
  3.4 0.7 %copy-done.3 = bf16[64,3,3,3,3]{0,4,3,2,1:T(4,128)(2,1)S(1)} copy-done((bf16[64,3,3,3,3]{0,4,3,2,1:T(4,128)(2,1)S(1)}, bf16[64,3,3,3,3]{0,4,3,2,1:T(4,128)(2,1)}, u32[]{:S(2)}) %copy-start.3) | copy-done | bytes 10392
  4.1 32.5 %shard_map.59 = (f32[192,128]{1,0:T(8,128)S(1)}, f32[384,128]{1,0:T(8,128)S(1)}) custom-call(f32[192,128]{1,0:T(8,128)S(1)} %bitcast.8, bf16[3,3,3,3,64]{4,3,2,1,0:T(4,128)(2,1)S(1)} %bitcast.11, bf16[3,3,3,64,64]{4,3,2,1,0:T(8,128)(2,1)S(1)} %bitcast.6, bf16[6,3,3,3,64]{4,3,2,1,0:T(4,128)(2,1)S(1)} %bitcast.10), custom_call_target="tpu_custom_call" | custom-call | tf_op jit(solution)/shard_map/pallas_call | solution.py:299
  36.6 0.6 %copy.8 = f32[3,4,16,128]{3,2,1,0:T(8,128)} copy(f32[3,4,16,128]{3,2,1,0:T(8,128)S(1)} %bitcast.9) | data formatting | bytes 196608
  37.2 0.7 %copy.9 = f32[6,4,16,128]{3,2,1,0:T(8,128)} copy(f32[6,4,16,128]{3,2,1,0:T(8,128)S(1)} %bitcast.7) | data formatting | bytes 393216
Async XLA Ops:
  0.6 1.0 %copy-start = (bf16[64,64,3,3,3]{1,0,4,3,2:T(8,128)(2,1)S(1)}, bf16[64,64,3,3,3]{1,0,4,3,2:T(8,128)(2,1)}, u32[]{:S(2)}) copy-start(bf16[64,64,3,3,3]{1,0,4,3,2:T(8,128)(2,1)} %param.6) | copy-start | bytes 663556
  1.6 0.9 %copy-start.1 = (f32[3,4,16,128]{3,2,1,0:T(8,128)S(1)}, f32[3,4,16,128]{3,2,1,0:T(8,128)}, u32[]{:S(2)}) copy-start(f32[3,4,16,128]{3,2,1,0:T(8,128)} %param.4) | copy-start | bytes 294916
  2.5 0.8 %copy-start.2 = (bf16[6,64,3,3,3]{1,4,3,2,0:T(4,128)(2,1)S(1)}, bf16[6,64,3,3,3]{1,4,3,2,0:T(4,128)(2,1)}, u32[]{:S(2)}) copy-start(bf16[6,64,3,3,3]{1,4,3,2,0:T(4,128)(2,1)} %param.7) | copy-start | bytes 62212
  3.4 0.7 %copy-start.3 = (bf16[64,3,3,3,3]{0,4,3,2,1:T(4,128)(2,1)S(1)}, bf16[64,3,3,3,3]{0,4,3,2,1:T(4,128)(2,1)}, u32[]{:S(2)}) copy-start(bf16[64,3,3,3,3]{0,4,3,2,1:T(4,128)(2,1)} %param.5) | copy-start | bytes 31108

commit v2 on v1

--- a/solution.py
+++ b/solution.py
@@ -39,7 +39,7 @@
 
 def kernel(
     vel_hbm, wi_hbm, wm_hbm, wo_hbm, ten_ref, str_ref,
-    v, hx, hy, ysend, uf, u16, wi_raw, wm_raw, wo_raw, wt0, wt1, wi, wp, wof, wo, h1, h2, q, ve, s, s16, ys16, sx, sy, se,
+    v, hx, hy, hd, ysend, ydiag, uf, u16, wi_raw, wm_raw, wo_raw, wt0, wt1, wi, wp, wof, wo, h1, h2, q, ve, s, s16, ys16, sx, sy, se,
     load_sem, send_a, recv_a, send_b, recv_b,
 ):
     n = 128
@@ -63,28 +63,32 @@
     for load in loads:
         load.start()
     v[pl.ds(192, 64), :] = jnp.zeros((64, 128), F32)
+
+    def remote(src, dst, k, send_sem, recv_sem):
+        copy = pltpu.make_async_remote_copy(
+            src_ref=src, dst_ref=dst, send_sem=send_sem.at[k], recv_sem=recv_sem.at[opposite[k]],
+            device_id=peers[k], device_id_type=MESH,
+        )
+        copy.start()
+        return copy
+
+    pl.semaphore_wait(barrier, 5)
+    vel3 = vel_hbm.reshape(3, 64, 128)
+    sends = [
+        remote(vel3.at[:, pl.ds(0, 48), :], hx.at[1], 0, send_a, recv_a),
+        remote(vel3.at[:, pl.ds(16, 48), :], hx.at[0], 1, send_a, recv_a),
+    ]
     loads[0].wait()
     near = 13 * (1 - gy)
     for r in range(3):
-        ysend[r] = v[pl.ds(near + r, 16, stride=16), :]
-    pl.semaphore_wait(barrier, 5)
-
-    v3 = v.at[pl.ds(0, 192)].reshape(3, 64, 128)
-    sends = []
-    for k in range(5):
-        if k == 0:
-            src, dst = v3.at[:, pl.ds(0, 48), :], hx.at[opposite[k]]
-        elif k == 1:
-            src, dst = v3.at[:, pl.ds(16, 48), :], hx.at[opposite[k]]
-        else:
-            src, dst = ysend, hy.at[opposite[k] - 2]
-        sends.append(
-            pltpu.make_async_remote_copy(
-                src_ref=src, dst_ref=dst, send_sem=send_a.at[k], recv_sem=recv_a.at[opposite[k]],
-                device_id=peers[k], device_id_type=MESH,
-            )
-        )
-        sends[-1].start()
+        row = v[pl.ds(near + r, 16, stride=16), :]
+        ysend[r] = row
+        ydiag[r] = row.astype(BF16)
+    sends += [
+        remote(ysend, hy, 2, send_a, recv_a),
+        remote(ydiag, hd.at[1], 3, send_a, recv_a),
+        remote(ydiag, hd.at[0], 4, send_a, recv_a),
+    ]
 
     @pl.loop(0, 10)
     def _(i):
@@ -95,9 +99,14 @@
             start = x * URO + (2 * gy + 1) * 16 + dz * 3 + c
             uf[pl.ds(start, 16, stride=16), :] = spin(field, 1 - dz)
 
+    def rounded(x):
+        u16[pl.ds(x * URO, URO), :] = uf[pl.ds(x * URO, URO), :].astype(BF16)
+
     for c in range(3):
         for x in range(4):
             patch(v[pl.ds((c * 4 + x) * 16, 16), :], x + 3, c)
+    for x in range(3, 7):
+        rounded(x)
 
     loads[1].wait()
     wt0[...] = jnp.zeros_like(wt0)
@@ -140,43 +149,32 @@
         q[dy, 0] = jnp.zeros((24, 128), F32)
         q[dy, 19] = jnp.zeros((24, 128), F32)
 
-    for k in range(5):
+    for k in range(2):
         sends[k].wait_recv()
-
-    for c in range(3):
+    for side, x_to in ((0, 0), (1, 7)):
         for x in range(3):
-            patch(hx[0, c, pl.ds(x * 16, 16), :], x, c)
-            patch(hx[1, c, pl.ds(x * 16, 16), :], x + 7, c)
-    far = jnp.where(gy == 0, 17, 0)
-    for r in range(3):
-        for side, x_from, x_to, count in ((0, 0, 3, 4), (1, 1, 0, 3), (2, 0, 7, 3)):
-            row = hy[side, r]
-            for dz in range(3):
-                turned = spin(row, 1 - dz)
-                for c in range(3):
-                    start = x_to * URO + (far + r) * 16 + dz * 3 + c
-                    uf[pl.ds(start, count, stride=URO), :] = turned[c * 4 + x_from:c * 4 + x_from + count]
-
-    @pl.loop(0, 10)
-    def _(i):
-        u16[pl.ds(i * URO, URO), :] = uf[pl.ds(i * URO, URO), :].astype(BF16)
-
-    @pl.loop(0, 9)
-    def _(t):
-        j = t * 2
+            for c in range(3):
+                patch(hx[side, c, pl.ds(x * 16, 16), :], x + x_to, c)
+    for x in (0, 1, 2, 7, 8, 9):
+        rounded(x)
+
+    def place(i):
+        return jnp.where(gy == 0, i, 8 - i) * 2
+
+    def layer1(i):
+        j = place(i)
         for p in range(4):
             def rows(dj):
                 return jnp.concatenate(
-                    [u16[pl.ds((2 * p + i) * URO + (j + dj) * 16, 48), :] for i in range(4)], axis=0
+                    [u16[pl.ds((2 * p + k) * URO + (j + dj) * 16, 48), :] for k in range(4)], axis=0
                 )
             out = gelu(jnp.dot(wi[...], jnp.concatenate([rows(0), rows(1)], axis=1), preferred_element_type=F32))
             out = out.astype(BF16)
             h1[j + 1, pl.ds(p * 128, 128), :] = out[:, :128]
             h1[j + 2, pl.ds(p * 128, 128), :] = out[:, 128:]
 
-    @pl.loop(0, 9)
-    def _(t):
-        j = t * 2
+    def layer2(i):
+        j = place(i)
         for p in range(3):
             def rows(dj):
                 return jnp.concatenate(
@@ -188,9 +186,8 @@
                 out = gelu(spin(half[0:128], 1) + half[128:256] + spin(half[256:384], -1))
                 h2[j + dj, pl.ds(p * 128, 128), :] = out.astype(BF16)
 
-    @pl.loop(0, 9)
-    def _(t):
-        j = t * 2
+    def layer3(i):
+        j = place(i)
         part = jnp.dot(wo[...], jnp.concatenate([h2[j], h2[j + 1]], axis=1), preferred_element_type=F32)
         for dj in range(2):
             half = part[:, dj * 128:dj * 128 + 128]
@@ -200,38 +197,69 @@
                     spin(half[at:at + 24], 1) + half[at + 24:at + 48] + spin(half[at + 48:at + 72], -1)
                 )
 
-    @pl.loop(0, 16)
-    def _(y):
-        j = y + 2 * gy
-        s[pl.ds(y, 24, stride=16), :] = q[0, j] + q[1, j + 1] + q[2, j + 2]
+    def gather(i):
+        j = place(i)
+        for dj in range(2):
+            total = q[0, j + dj] + q[1, j + dj + 1] + q[2, j + dj + 2]
+            s[pl.ds(j + dj - 2 * gy, 24, stride=16), :] = total
+
+    layer1(0)
+    layer1(1)
+    layer1(2)
+    layer2(0)
+
+    @pl.loop(3, 7)
+    def _(i):
+        layer3(i - 3)
+        layer2(i - 2)
+        layer1(i)
+
+    for k in range(2, 5):
+        sends[k].wait_recv()
+    far = jnp.where(gy == 0, 17, 0)
+    for r in range(3):
+        for row, x_from, x_to, count in (
+            (hy[r], 0, 3, 4), (hd[0, r].astype(F32), 1, 0, 3), (hd[1, r].astype(F32), 0, 7, 3)
+        ):
+            for dz in range(3):
+                turned = spin(row, 1 - dz)
+                for c in range(3):
+                    start = x_to * URO + (far + r) * 16 + dz * 3 + c
+                    uf[pl.ds(start, count, stride=URO), :] = turned[c * 4 + x_from:c * 4 + x_from + count]
+    for x in range(10):
+        at = x * URO + far * 16
+        u16[pl.ds(at, 48), :] = uf[pl.ds(at, 48), :].astype(BF16)
+
+    @pl.loop(7, 9)
+    def _(i):
+        layer3(i - 3)
+        layer2(i - 2)
+        layer1(i)
+        gather(i - 7)
+
+    layer3(6)
+    layer2(7)
+    gather(2)
+    gather(3)
+    layer3(7)
+    layer2(8)
+    gather(4)
+    gather(5)
+    layer3(8)
+    gather(6)
+    gather(7)
 
     for k in range(3):
         s16[k] = s[pl.ds(k * 64, 64), :].astype(BF16)
+    last = [
+        remote(s16.at[:, pl.ds(0, 48), :], sx.at[1], 0, send_b, recv_b),
+        remote(s16.at[:, pl.ds(16, 48), :], sx.at[0], 1, send_b, recv_b),
+    ]
     for r in range(3):
         ys16[r] = s[pl.ds(128 + near + r, 16, stride=16), :].astype(BF16)
-    last = []
-    for k in range(3):
-        if k == 0:
-            src, dst = s16.at[:, pl.ds(0, 48), :], sx.at[1]
-        elif k == 1:
-            src, dst = s16.at[:, pl.ds(16, 48), :], sx.at[0]
-        else:
-            src, dst = ys16, sy
-        last.append(
-            pltpu.make_async_remote_copy(
-                src_ref=src, dst_ref=dst, send_sem=send_b.at[k], recv_sem=recv_b.at[opposite[k]],
-                device_id=peers[k], device_id_type=MESH,
-            )
-        )
-        last[-1].start()
+    last.append(remote(ys16, sy, 2, send_b, recv_b))
 
     low_side = gy == 1
-
-    def edge(ext, halo, count):
-        for r in range(3):
-            row = halo(r)
-            ext[pl.ds(24 + r, count, stride=32), :] = jnp.where(low_side, 0.0, row)
-            ext[pl.ds(5 + r, count, stride=32), :] = jnp.where(low_side, row, 0.0)
 
     def x_plane(c, x):
         if x < 0:
@@ -240,15 +268,31 @@
             return hx[1, c, pl.ds((x - 4) * 16, 16), :]
         return v[pl.ds((c * 4 + x) * 16, 16), :]
 
+    def s_plane(k, x):
+        if x < 0:
+            return sx[0, k, pl.ds((x + 3) * 16, 16), :].astype(F32)
+        if x > 3:
+            return sx[1, k, pl.ds((x - 4) * 16, 16), :].astype(F32)
+        return s[pl.ds((k * 4 + x) * 16, 16), :]
+
     for i in range(12):
         ve[pl.ds(i * 32 + 8, 16), :] = v[pl.ds(i * 16, 16), :]
-    edge(ve, lambda r: hy[0, r, pl.ds(0, 12), :], 12)
-    for c in range(3):
+        se[pl.ds(i * 32, 8), :] = jnp.zeros((8, 128), F32)
+        se[pl.ds(i * 32 + 8, 16), :] = s[pl.ds(128 + i * 16, 16), :]
+        se[pl.ds(i * 32 + 24, 8), :] = jnp.zeros((8, 128), F32)
+    for r in range(3):
+        row = hy[r, pl.ds(0, 12), :]
+        ve[pl.ds(24 + r, 12, stride=32), :] = jnp.where(low_side, 0.0, row)
+        ve[pl.ds(5 + r, 12, stride=32), :] = jnp.where(low_side, row, 0.0)
+    parts = ((0, 0, 1), (2, 1, 4), (1, 2, 5))
+    for c, (along_x, along_y, along_z) in enumerate(parts):
         for x in range(4):
             mid = x_plane(c, x)
+            edge = s_plane(along_z, x)
             base = (c * 4 + x) * 32 + 8
             d1 = [0.0, 0.0, 0.0]
             d2 = (3.0 * CENTER) * mid
+            div = 0.0
             for k in range(3):
                 pairs = (
                     (x_plane(c, x + k + 1), x_plane(c, x - k - 1)),
@@ -258,54 +302,67 @@
                 for a, (up, down) in enumerate(pairs):
                     d1[a] = d1[a] + A1[k] * (up - down)
                     d2 = d2 + A2[k] * (up + down)
+                inner = (
+                    (se[pl.ds(base + k + 1, 16), :] - se[pl.ds(base - k - 1, 16), :])
+                    + (spin(edge, -k - 1) - spin(edge, k + 1))
+                )
+                if x + k + 1 < 4:
+                    inner = inner + s_plane(along_x, x + k + 1)
+                if x - k - 1 >= 0:
+                    inner = inner - s_plane(along_x, x - k - 1)
+                div = div + A1[k] * inner
             advect = x_plane(0, x) * d1[0] + x_plane(1, x) * d1[1] + x_plane(2, x) * d1[2]
-            ten_ref[pl.ds((c * 4 + x) * 16, 16), :] = 0.2 * d2 - advect
+            ten_ref[pl.ds((c * 4 + x) * 16, 16), :] = 0.2 * d2 - advect - div
     for k in range(6):
         str_ref[pl.ds(ORDER[k] * 64, 64), :] = s[pl.ds(k * 64, 64), :]
-    for i in range(12):
-        se[pl.ds(i * 32 + 8, 16), :] = s[pl.ds(128 + i * 16, 16), :]
-
-    for k in range(3):
+
+    last[2].wait_recv()
+    rim = [sy[r].astype(F32)[:12] for r in range(3)]
+    up = (
+        A1[2] * rim[0],
+        A1[1] * rim[0] + A1[2] * rim[1],
+        A1[0] * rim[0] + A1[1] * rim[1] + A1[2] * rim[2],
+    )
+    down = (
+        A1[0] * rim[2] + A1[1] * rim[1] + A1[2] * rim[0],
+        A1[1] * rim[2] + A1[2] * rim[1],
+        A1[2] * rim[2],
+    )
+    for r in range(3):
+        at = pl.ds(near + r, 12, stride=16)
+        ten_ref[at, :] = ten_ref[at, :] + jnp.where(low_side, down[r], -up[r])
+    for k in range(2):
         last[k].wait_recv()
-
-    def s_plane(k, x):
-        if x < 0:
-            return sx[0, k, pl.ds((x + 3) * 16, 16), :].astype(F32)
-        if x > 3:
-            return sx[1, k, pl.ds((x - 4) * 16, 16), :].astype(F32)
-        return s[pl.ds((k * 4 + x) * 16, 16), :]
-
-    edge(se, lambda r: sy[r].astype(F32)[:12], 12)
-    for c, (along_x, along_y, along_z) in enumerate(((0, 0, 1), (2, 1, 4), (1, 2, 5))):
+    for c, (along_x, _, _) in enumerate(parts):
         for x in range(4):
-            base = (along_y * 4 + x) * 32 + 8
-            mid = s[pl.ds((along_z * 4 + x) * 16, 16), :]
-            total = ten_ref[pl.ds((c * 4 + x) * 16, 16), :]
+            at = pl.ds((c * 4 + x) * 16, 16)
+            total = ten_ref[at, :]
             for k in range(3):
-                total = total - A1[k] * (
-                    (s_plane(along_x, x + k + 1) - s_plane(along_x, x - k - 1))
-                    + (se[pl.ds(base + k + 1, 16), :] - se[pl.ds(base - k - 1, 16), :])
-                    + (spin(mid, -k - 1) - spin(mid, k + 1))
-                )
-            ten_ref[pl.ds((c * 4 + x) * 16, 16), :] = total
+                if x + k + 1 > 3:
+                    total = total - A1[k] * s_plane(along_x, x + k + 1)
+                if x - k - 1 < 0:
+                    total = total + A1[k] * s_plane(along_x, x - k - 1)
+            ten_ref[at, :] = total
 
     for send in sends + last:
         send.wait_send()
 
 
 def shards(velocity, kernel_in, kernel_mid, kernel_out):
-    anywhere = pl.BlockSpec(memory_space=pl.ANY)
+    anywhere = pl.BlockSpec(memory_space=pltpu.HBM)
     whole = pl.BlockSpec(memory_space=pltpu.VMEM)
     tendency, stress = pl.pallas_call(
         kernel,
-        out_shape=(jax.ShapeDtypeStruct((192, 128), F32), jax.ShapeDtypeStruct((384, 128), F32)),
+        out_shape=(pltpu.VMEM((192, 128), F32), pltpu.VMEM((384, 128), F32)),
         in_specs=[anywhere] * 4,
         out_specs=(whole, whole),
         scratch_shapes=[
             pltpu.VMEM((256, 128), F32),
             pltpu.VMEM((2, 3, 48, 128), F32),
-            pltpu.VMEM((3, 3, 16, 128), F32),
             pltpu.VMEM((3, 16, 128), F32),
+            pltpu.VMEM((2, 3, 16, 128), BF16),
+            pltpu.VMEM((3, 16, 128), F32),
+            pltpu.VMEM((3, 16, 128), BF16),
             pltpu.VMEM((10 * URO, 128), F32),
             pltpu.VMEM((10 * URO, 128), BF16),
             pltpu.VMEM((3, 3, 3, 3, 64), BF16),
@@ -334,7 +391,7 @@
             pltpu.SemaphoreType.DMA((3,)),
         ],
         compiler_params=pltpu.CompilerParams(
-            collective_id=0, has_side_effects=True, vmem_limit_bytes=48 * 1024 * 1024
+            collective_id=0, has_side_effects=True, vmem_limit_bytes=60 * 1024 * 1024
         ),
     )(
         velocity.reshape(192, 128),

time: 38.5 us -> 30.2 us (0.78); the launches traced: 37.9 us -> 30.1 us
  Pallas kernels: 32.5 us -> 28.1 us
  local copies, waits for them, and re-layouts: 4.78 us -> 1.32 us
    pallas_call x1, Pallas kernels: 32.5 us -> 28.1 us  [shards(): pl.pallas_call(kernel, out_shape=(pltpu.VMEM((192, 128), F32), pltpu.VMEM...]
    unnamed x10 -> x2, local copies, waits for them, and re-layouts: 4.78 us -> 1.32 us
where the time goes in v2:
time: 30.2 us; the launch traced here: 30.1 us
  Pallas kernels  28.1 us (93%)
  local copies, waits for them, and re-layouts  1.32 us (4%)
  between operations  0.64 us (2%)
    pallas_call x1, Pallas kernels, shards(): pl.pallas_call(kernel, out_shape=(pltpu.VMEM((192, 128), F32), pltpu.VMEM...  28.1 us
    unnamed x2, local copies, waits for them, and re-layouts  1.32 us

profile of v2, /device:TPU:2, one launch (start us, length us, event | category | flops | bytes accessed | tf_op | source)
XLA Modules:
  0.0 30.1 jit_solution(3978416072079427570)
XLA Ops:
  0.6 28.1 %shard_map.59 = (f32[192,128]{1,0:T(8,128)S(1)}, f32[384,128]{1,0:T(8,128)S(1)}) custom-call(f32[192,128]{1,0:T(8,128)} %bitcast.9, bf16[3,3,3,3,64]{4,3,2,1,0:T(4,128)(2,1)} %bitcast.11, bf16[3,3,3,64,64]{4,3,2,1,0:T(8,128)(2,1)} %bitcast.8, bf16[6,3,3,3,64]{4,3,2,1,0:T(4,128)(2,1)} %bitcast.10), custom_call_target="tpu_custom_call" | custom-call | tf_op jit(solution)/shard_map/pallas_call | solution.py:354
  28.8 0.6 %copy.8 = f32[3,4,16,128]{3,2,1,0:T(8,128)} copy(f32[3,4,16,128]{3,2,1,0:T(8,128)S(1)} %bitcast.7) | data formatting | bytes 196608
  29.4 0.7 %copy.9 = f32[6,4,16,128]{3,2,1,0:T(8,128)} copy(f32[6,4,16,128]{3,2,1,0:T(8,128)S(1)} %bitcast.6) | data formatting | bytes 393216

commit v3 on v2

--- a/solution.py
+++ b/solution.py
@@ -108,6 +108,9 @@
     for x in range(3, 7):
         rounded(x)
 
+    def outward(dy):
+        return jnp.where(gy == 0, dy, 2 - dy)
+
     loads[1].wait()
     wt0[...] = jnp.zeros_like(wt0)
     wt1[...] = jnp.zeros_like(wt1)
@@ -124,7 +127,7 @@
     loads[2].wait()
     for dy in range(3):
         for dz in range(3):
-            a, b, c, d = band(wm_raw[0, dy, dz], wm_raw[1, dy, dz], wm_raw[2, dy, dz])
+            a, b, c, d = band(*(wm_raw[dx, outward(dy), dz] for dx in range(3)))
             wp[pl.ds(dz * 128, 64), pl.ds(dy * 256, 128)] = a
             wp[pl.ds(dz * 128, 64), pl.ds(dy * 256 + 128, 128)] = b
             wp[pl.ds(dz * 128 + 64, 64), pl.ds(dy * 256, 128)] = c
@@ -134,7 +137,7 @@
     wof[...] = jnp.zeros_like(wof)
     for k in range(6):
         for dy in range(3):
-            a, b, c, d = band(*(wo_raw[ORDER[k], dx, dy].astype(F32) for dx in range(3)))
+            a, b, c, d = band(*(wo_raw[ORDER[k], dx, outward(dy)].astype(F32) for dx in range(3)))
             for x in range(4):
                 first, second = ((a, b), (c, d))[x % 2]
                 rows = pl.ds(dy * 72 + k * 4 + x, 3, stride=24)
@@ -158,61 +161,61 @@
     for x in (0, 1, 2, 7, 8, 9):
         rounded(x)
 
-    def place(i):
-        return jnp.where(gy == 0, i, 8 - i) * 2
-
-    def layer1(i):
-        j = place(i)
-        for p in range(4):
-            def rows(dj):
-                return jnp.concatenate(
-                    [u16[pl.ds((2 * p + k) * URO + (j + dj) * 16, 48), :] for k in range(4)], axis=0
-                )
-            out = gelu(jnp.dot(wi[...], jnp.concatenate([rows(0), rows(1)], axis=1), preferred_element_type=F32))
-            out = out.astype(BF16)
-            h1[j + 1, pl.ds(p * 128, 128), :] = out[:, :128]
-            h1[j + 2, pl.ds(p * 128, 128), :] = out[:, 128:]
-
-    def layer2(i):
-        j = place(i)
-        for p in range(3):
-            def rows(dj):
-                return jnp.concatenate(
-                    [h1[j + dj + dy, pl.ds(p * 128, 256), :] for dy in range(3)], axis=0
-                )
-            part = jnp.dot(wp[...], jnp.concatenate([rows(0), rows(1)], axis=1), preferred_element_type=F32)
-            for dj in range(2):
-                half = part[:, dj * 128:dj * 128 + 128]
-                out = gelu(spin(half[0:128], 1) + half[128:256] + spin(half[256:384], -1))
-                h2[j + dj, pl.ds(p * 128, 128), :] = out.astype(BF16)
+    def layer1(i, p):
+        def rows(e):
+            j = jnp.where(gy == 0, 2 * i + e, 17 - 2 * i - e)
+            return jnp.concatenate(
+                [u16[pl.ds((2 * p + k) * URO + j * 16, 48), :] for k in range(4)], axis=0
+            )
+        out = gelu(jnp.dot(wi[...], jnp.concatenate([rows(0), rows(1)], axis=1), preferred_element_type=F32))
+        out = out.astype(BF16)
+        h1[2 * i + 1, pl.ds(p * 128, 128), :] = out[:, :128]
+        h1[2 * i + 2, pl.ds(p * 128, 128), :] = out[:, 128:]
+
+    def layer2(i, p):
+        def rows(e):
+            return jnp.concatenate(
+                [h1[2 * i + e + dy, pl.ds(p * 128, 256), :] for dy in range(3)], axis=0
+            )
+        part = jnp.dot(wp[...], jnp.concatenate([rows(0), rows(1)], axis=1), preferred_element_type=F32)
+        for e in range(2):
+            half = part[:, e * 128:e * 128 + 128]
+            out = gelu(spin(half[0:128], 1) + half[128:256] + spin(half[256:384], -1))
+            h2[2 * i + e, pl.ds(p * 128, 128), :] = out.astype(BF16)
 
     def layer3(i):
-        j = place(i)
-        part = jnp.dot(wo[...], jnp.concatenate([h2[j], h2[j + 1]], axis=1), preferred_element_type=F32)
-        for dj in range(2):
-            half = part[:, dj * 128:dj * 128 + 128]
+        part = jnp.dot(wo[...], jnp.concatenate([h2[2 * i], h2[2 * i + 1]], axis=1), preferred_element_type=F32)
+        for e in range(2):
+            half = part[:, e * 128:e * 128 + 128]
             for dy in range(3):
                 at = dy * 72
-                q[dy, j + dj + 1] = (
+                q[dy, 2 * i + e + 1] = (
                     spin(half[at:at + 24], 1) + half[at + 24:at + 48] + spin(half[at + 48:at + 72], -1)
                 )
 
     def gather(i):
-        j = place(i)
-        for dj in range(2):
-            total = q[0, j + dj] + q[1, j + dj + 1] + q[2, j + dj + 2]
-            s[pl.ds(j + dj - 2 * gy, 24, stride=16), :] = total
-
-    layer1(0)
-    layer1(1)
-    layer1(2)
-    layer2(0)
+        for e in range(2):
+            d = 2 * i + e
+            total = q[0, d] + q[1, d + 1] + q[2, d + 2]
+            s[pl.ds(jnp.where(gy == 0, d, 15 - d), 24, stride=16), :] = total
+
+    def step(first, second, third, gathered=()):
+        for p in range(4):
+            if second is not None and p < 3:
+                layer2(second, p)
+            if first is not None:
+                layer1(first, p)
+            if third is not None and p == 2:
+                layer3(third)
+        for i in gathered:
+            gather(i)
+    step(0, None, None)
+    step(1, None, None)
+    step(2, 0, None)
 
     @pl.loop(3, 7)
     def _(i):
-        layer3(i - 3)
-        layer2(i - 2)
-        layer1(i)
+        step(i, i - 2, i - 3)
 
     for k in range(2, 5):
         sends[k].wait_recv()
@@ -232,22 +235,11 @@
 
     @pl.loop(7, 9)
     def _(i):
-        layer3(i - 3)
-        layer2(i - 2)
-        layer1(i)
-        gather(i - 7)
-
-    layer3(6)
-    layer2(7)
-    gather(2)
-    gather(3)
-    layer3(7)
-    layer2(8)
-    gather(4)
-    gather(5)
-    layer3(8)
-    gather(6)
-    gather(7)
+        step(i, i - 2, i - 3, (i - 7,))
+
+    step(None, 7, 6, (2, 3))
+    step(None, 8, 7, (4, 5))
+    step(None, None, 8, (6, 7))
 
     for k in range(3):
         s16[k] = s[pl.ds(k * 64, 64), :].astype(BF16)
@@ -346,6 +338,17 @@
 
     for send in sends + last:
         send.wait_send()
+
+
+def emit(ten_vmem, str_vmem, ten_hbm, str_hbm, sem):
+    copies = [
+        pltpu.make_async_copy(str_vmem, str_hbm, sem.at[0]),
+        pltpu.make_async_copy(ten_vmem, ten_hbm, sem.at[1]),
+    ]
+    for copy in copies:
+        copy.start()
+    for copy in copies:
+        copy.wait()
 
 
 def shards(velocity, kernel_in, kernel_mid, kernel_out):
@@ -399,6 +402,15 @@
         jnp.transpose(kernel_mid, (2, 3, 4, 0, 1)),
         jnp.transpose(kernel_out, (0, 2, 3, 4, 1)),
     )
+    free = pl.BlockSpec(memory_space=pl.ANY)
+    tendency, stress = pl.pallas_call(
+        emit,
+        out_shape=(jax.ShapeDtypeStruct((192, 128), F32), jax.ShapeDtypeStruct((384, 128), F32)),
+        in_specs=(free, free),
+        out_specs=(free, free),
+        scratch_shapes=[pltpu.SemaphoreType.DMA((2,))],
+        compiler_params=pltpu.CompilerParams(vmem_limit_bytes=1024 * 1024),
+    )(tendency, stress)
     return tendency.reshape(3, 4, 16, 128), stress.reshape(6, 4, 16, 128)
 
 

time: 30.2 us -> 28.9 us (0.957)
  local copies, waits for them, and re-layouts: 1.32 us -> 0 us
    unnamed x2 -> x0, local copies, waits for them, and re-layouts: 1.32 us -> none
    pallas_call x1, Pallas kernels: 28.1 us -> 27.4 us  [shards(): pl.pallas_call(kernel, out_shape=(pltpu.VMEM((192, 128), F32), pltpu.VMEM...]
    pallas_call x0 -> x1, Pallas kernels: none -> 0.72 us  [shards(): pl.pallas_call(emit, out_shape=(jax.ShapeDtypeStruct((192, 128), F32), ja...]
where the time goes in v3:
time: 28.9 us; the launch traced here: 28.8 us
  Pallas kernels  28.1 us (97%)
  between operations  0.64 us (2%)
    pallas_call x1, Pallas kernels, shards(): pl.pallas_call(kernel, out_shape=(pltpu.VMEM((192, 128), F32), pltpu.VMEM...  27.4 us
    pallas_call x1, Pallas kernels, shards(): pl.pallas_call(emit, out_shape=(jax.ShapeDtypeStruct((192, 128), F32), ja...  0.72 us

profile of v3, /device:TPU:2, one launch (start us, length us, event | category | flops | bytes accessed | tf_op | source)
XLA Modules:
  0.0 28.8 jit_solution(10377782824474640951)
XLA Ops:
  0.6 27.4 %shard_map.59 = (f32[192,128]{1,0:T(8,128)S(1)}, f32[384,128]{1,0:T(8,128)S(1)}) custom-call(f32[192,128]{1,0:T(8,128)} %bitcast.7, bf16[3,3,3,3,64]{4,3,2,1,0:T(4,128)(2,1)} %bitcast.9, bf16[3,3,3,64,64]{4,3,2,1,0:T(8,128)(2,1)} %bitcast.6, bf16[6,3,3,3,64]{4,3,2,1,0:T(4,128)(2,1)} %bitcast.8), custom_call_target="tpu_custom_call" | custom-call | tf_op jit(solution)/shard_map/pallas_call | solution.py:357
  28.0 0.7 %shard_map.60 = (f32[192,128]{1,0:T(8,128)}, f32[384,128]{1,0:T(8,128)}) custom-call(f32[192,128]{1,0:T(8,128)S(1)} %get-tuple-element.6.ten_vmem, f32[384,128]{1,0:T(8,128)S(1)} %get-tuple-element.7.str_vmem), custom_call_target="tpu_custom_call" | custom-call | tf_op jit(solution)/shard_map/pallas_call | solution.py:406

commit v4 on v3

--- a/solution.py
+++ b/solution.py
@@ -183,6 +183,24 @@
             out = gelu(spin(half[0:128], 1) + half[128:256] + spin(half[256:384], -1))
             h2[2 * i + e, pl.ds(p * 128, 128), :] = out.astype(BF16)
 
+    def layer2_last():
+        for places in ((0, 1), (2,)):
+            rhs = [
+                jnp.concatenate([h1[16 + dy, pl.ds(p * 128, 256), :] for dy in range(3)], axis=0) for p in places
+            ]
+            rhs = jnp.concatenate(rhs, axis=1) if len(places) > 1 else rhs[0]
+            part = jnp.dot(wp[...], rhs, preferred_element_type=F32)
+            for k, p in enumerate(places):
+                half = part[:, k * 128:k * 128 + 128]
+                out = gelu(spin(half[0:128], 1) + half[128:256] + spin(half[256:384], -1))
+                h2[16, pl.ds(p * 128, 128), :] = out.astype(BF16)
+
+    def layer3_last():
+        half = jnp.dot(wo[...], h2[16], preferred_element_type=F32)
+        for dy in range(3):
+            at = dy * 72
+            q[dy, 17] = spin(half[at:at + 24], 1) + half[at + 24:at + 48] + spin(half[at + 48:at + 72], -1)
+
     def layer3(i):
         part = jnp.dot(wo[...], jnp.concatenate([h2[2 * i], h2[2 * i + 1]], axis=1), preferred_element_type=F32)
         for e in range(2):
@@ -213,8 +231,7 @@
     step(1, None, None)
     step(2, 0, None)
 
-    @pl.loop(3, 7)
-    def _(i):
+    for i in range(3, 7):
         step(i, i - 2, i - 3)
 
     for k in range(2, 5):
@@ -233,13 +250,15 @@
         at = x * URO + far * 16
         u16[pl.ds(at, 48), :] = uf[pl.ds(at, 48), :].astype(BF16)
 
-    @pl.loop(7, 9)
-    def _(i):
+    for i in range(7, 9):
         step(i, i - 2, i - 3, (i - 7,))
 
     step(None, 7, 6, (2, 3))
-    step(None, 8, 7, (4, 5))
-    step(None, None, 8, (6, 7))
+    layer2_last()
+    step(None, None, 7, (4, 5))
+    layer3_last()
+    gather(6)
+    gather(7)
 
     for k in range(3):
         s16[k] = s[pl.ds(k * 64, 64), :].astype(BF16)
@@ -378,7 +397,7 @@
             pltpu.VMEM((3, 216, 128), F32),
             pltpu.VMEM((216, 384), BF16),
             pltpu.VMEM((20, 512, 128), BF16),
-            pltpu.VMEM((18, 384, 128), BF16),
+            pltpu.VMEM((17, 384, 128), BF16),
             pltpu.VMEM((3, 20, 24, 128), F32),
             pltpu.VMEM((12 * 32, 128), F32),
             pltpu.VMEM((384, 128), F32),

time: 28.9 us -> 26.9 us (0.931)
  Pallas kernels: 28.1 us -> 26.2 us
    pallas_call x1, Pallas kernels: 27.4 us -> 25.5 us  [shards(): pl.pallas_call(kernel, out_shape=(pltpu.VMEM((192, 128), F32), pltpu.VMEM...]
where the time goes in v4:
time: 26.9 us; the launch traced here: 26.8 us
  Pallas kernels  26.2 us (97%)
  between operations  0.64 us (2%)
    pallas_call x1, Pallas kernels, shards(): pl.pallas_call(kernel, out_shape=(pltpu.VMEM((192, 128), F32), pltpu.VMEM...  25.5 us
    pallas_call x1, Pallas kernels, shards(): pl.pallas_call(emit, out_shape=(jax.ShapeDtypeStruct((192, 128), F32), ja...  0.72 us

profile of v4, /device:TPU:2, one launch (start us, length us, event | category | flops | bytes accessed | tf_op | source)
XLA Modules:
  0.0 26.8 jit_solution(14097664265560506183)
XLA Ops:
  0.6 25.5 %shard_map.59 = (f32[192,128]{1,0:T(8,128)S(1)}, f32[384,128]{1,0:T(8,128)S(1)}) custom-call(f32[192,128]{1,0:T(8,128)} %bitcast.7, bf16[3,3,3,3,64]{4,3,2,1,0:T(4,128)(2,1)} %bitcast.9, bf16[3,3,3,64,64]{4,3,2,1,0:T(8,128)(2,1)} %bitcast.6, bf16[6,3,3,3,64]{4,3,2,1,0:T(4,128)(2,1)} %bitcast.8), custom_call_target="tpu_custom_call" | custom-call | tf_op jit(solution)/shard_map/pallas_call | solution.py:376
  26.1 0.7 %shard_map.60 = (f32[192,128]{1,0:T(8,128)}, f32[384,128]{1,0:T(8,128)}) custom-call(f32[192,128]{1,0:T(8,128)S(1)} %get-tuple-element.6.ten_vmem, f32[384,128]{1,0:T(8,128)S(1)} %get-tuple-element.7.str_vmem), custom_call_target="tpu_custom_call" | custom-call | tf_op jit(solution)/shard_map/pallas_call | solution.py:425
